TPU v7x, 32 devices: a whole 2x2x4 slice. The times are simulated.
32 devices in a mesh: dp: 8 (over z, x), seq: 4 (over y, core).
Axes of the slice: x: 2, y: 2, z: 4, core: 2. Of those that a mesh axis runs over, the one named last changes fastest.
Arguments:
- codes: int32 [8, 8192], P('dp', 'seq'), may hold values from 0 to 3
- embed: bfloat16 [4, 256], replicated, may hold values from -6 to 6
- first_weight_taps: bfloat16 [3, 256, 256], replicated, may hold values from -0.21875 to 0.21875
- second_weight_taps: bfloat16 [3, 256, 256], replicated, may hold values from -0.21875 to 0.21875
- cotangent: bfloat16 [8, 8192, 256], P('dp', 'seq'), may hold values from -6 to 6
Outputs:
- block_out: bfloat16 [8, 8192, 256], P('dp', 'seq')
- first_weight_gradient: float32 [3, 256, 256], replicated
- second_weight_gradient: float32 [3, 256, 256], replicated
All inputs are finite; a program needn't handle non-finite values.
Results may differ from a plain program's by a relative error of at most 0.0085.
Values may be sent and summed in bfloat16 or wider, within the bound.
A program may use at most 64 MiB of HBM per device.

v0:
```python
import jax
import jax.numpy as jnp
from jax import lax
from jax.sharding import PartitionSpec as P

FIRST_DILATION = 4
SECOND_DILATION = 16


def with_halo(cells, sides, width):
    for axis, dim in sides:
        count = lax.axis_size(axis)
        ends = count - 1
        head = lax.slice_in_dim(cells, 0, width, axis=dim)
        tail = lax.slice_in_dim(cells, cells.shape[dim] - width, cells.shape[dim], axis=dim)
        cells = jnp.concatenate(
            [
                lax.ppermute(tail, axis, [(i, (i + 1) % count) for i in range(ends)]),
                cells,
                lax.ppermute(head, axis, [((i + 1) % count, i) for i in range(ends)]),
            ],
            axis=dim,
        )
    return cells


def pad_rows(value, dilation):
    return with_halo(value, (("seq", 1),), dilation)


def stack_rows(padded, dilation, order):
    count_rows = padded.shape[1] - 2 * dilation
    return jnp.concatenate(
        [padded[:, k * dilation : k * dilation + count_rows] for k in order], axis=-1
    )


def product(stacked, matrix):
    shape_in = stacked.shape
    result = jnp.dot(stacked.reshape(-1, shape_in[-1]), matrix, preferred_element_type=jnp.float32)
    return result.reshape(shape_in[:-1] + (matrix.shape[1],))


def weight_term(stacked, grad):
    channels = grad.shape[-1]
    term = jnp.dot(
        stacked.reshape(-1, 3 * channels).T,
        grad.reshape(-1, channels),
        preferred_element_type=jnp.float32,
    )
    return term.reshape(3, channels, channels)


def layer_forward_pass(value, weight, dilation):
    channels = weight.shape[2]
    stacked = stack_rows(pad_rows(value, dilation), dilation, (0, 1, 2))
    flat = weight.reshape(-1, channels)
    reversed_taps = weight[::-1, ::-1, ::-1].reshape(-1, channels)
    both = product(stacked, jnp.concatenate([flat, reversed_taps], axis=1))
    return (both[..., :channels] + both[..., channels:], stacked)


def input_backward_pass(grad, weight, dilation):
    channels = weight.shape[2]
    stacked = stack_rows(pad_rows(grad, dilation), dilation, (2, 1, 0))
    flat_t = jnp.transpose(weight, (0, 2, 1)).reshape(-1, channels)
    reversed_t = jnp.transpose(weight[::-1, ::-1, ::-1], (0, 2, 1)).reshape(-1, channels)
    both = product(stacked, jnp.concatenate([flat_t, reversed_t], axis=1))
    return both[..., :channels] + both[..., channels:]


def strand_total(stacked, grad):
    term = weight_term(stacked, grad)
    return term + term[::-1, ::-1, ::-1]


def local(codes, embed, first_weight_taps, second_weight_taps, cotangent):
    onehot = (codes[..., None] == jnp.arange(4, dtype=jnp.int32)).astype(jnp.bfloat16)
    nucleotide_features = product(onehot, embed).astype(jnp.bfloat16)
    first_activation, first_shift_stack = layer_forward_pass(
        nucleotide_features, first_weight_taps, FIRST_DILATION
    )
    gelu_one, back_one = jax.vjp(jax.nn.gelu, first_activation)
    hidden_state = gelu_one.astype(jnp.bfloat16)
    second_activation, second_shift_stack = layer_forward_pass(
        hidden_state, second_weight_taps, SECOND_DILATION
    )
    gelu_two, back_two = jax.vjp(jax.nn.gelu, second_activation)
    block_out = (hidden_state.astype(jnp.float32) + gelu_two).astype(jnp.bfloat16)
    cotangent_wide_float = cotangent.astype(jnp.float32)
    second_activation_gradient = back_two(cotangent_wide_float)[0].astype(jnp.bfloat16)
    input_contribution = input_backward_pass(
        second_activation_gradient, second_weight_taps, SECOND_DILATION
    )
    second_weight_gradient = strand_total(second_shift_stack, second_activation_gradient)
    second_weight_gradient = lax.psum(second_weight_gradient, ("dp", "seq"))
    hidden_gradient = cotangent_wide_float + input_contribution
    first_activation_gradient = back_one(hidden_gradient)[0].astype(jnp.bfloat16)
    first_weight_gradient = strand_total(first_shift_stack, first_activation_gradient)
    first_weight_gradient = lax.psum(first_weight_gradient, ("dp", "seq"))
    return (block_out, first_weight_gradient, second_weight_gradient)


def solution(mesh):
    in_specs = (P("dp", "seq"), P(), P(), P(), P("dp", "seq", None))
    out_specs = (P("dp", "seq", None), P(), P())
    return jax.shard_map(local, mesh=mesh, in_specs=in_specs, out_specs=out_specs, check_vma=False)
```

profile of v0, /device:TPU:0, one launch (start us, length us, event | category | flops | bytes accessed | tf_op | source)
XLA Modules:
  0.0 223.1 jit_solution(89237702138022745)
XLA Ops:
  7.9 1.2 fusion.14
  9.1 1.3 collective-permute-start.1
  10.4 3.0 %collective-permute-start = (bf16[1,4,256]{2,1,0:T(4,128)(2,1)S(1)}, bf16[1,4,256]{2,1,0:T(4,128)(2,1)S(1)}, u32[]{:S(2)}, u32[]{:S(2)}) collective-permute-start(bf16[1,4,256]{2,1,0:T(4,128)(2,1)S(1)} %get-tuple-element.11), channel_id=1, source_target_pairs={{0,1},{1,2},{2,3},{4,5},{5,6},{6,7},{8,9},{9,10},{10,11},{12,13},{... | collective-permute-start | bytes 6152 | tf_op jit(solution)/shard_map/ppermute | solution.py:18
  13.4 5.3 %rev.14 = bf16[3,256,256]{2,1,0:T(8,128)(2,1)S(1)} reverse(bf16[3,256,256]{2,1,0:T(8,128)(2,1)} %param.8), dimensions={0,1,2} | reverse | bytes 786432 | tf_op jit(solution)/shard_map/rev | solution.py:58
  19.7 1.3 rev.13
  21.9 1.8 convolution_bitcast_fusion.2
  24.6 1.2 copy-done.1
  26.4 1.3 collective-permute-start.3
  27.7 5.7 %collective-permute-start.2 = (bf16[1,16,256]{2,1,0:T(8,128)(2,1)}, bf16[1,16,256]{2,1,0:T(8,128)(2,1)}, u32[]{:S(2)}, u32[]{:S(2)}) collective-permute-start(bf16[1,16,256]{2,1,0:T(8,128)(2,1)} %get-tuple-element.9), channel_id=1, source_target_pairs={{0,1},{1,2},{2,3},{4,5},{5,6},{6,7},{8,9},{9,10},{10,11},{12,13},{... | collective-permute-start | bytes 24584 | tf_op jit(solution)/shard_map/ppermute | solution.py:18
  33.4 4.4 %fusion.37 = bf16[768,2048]{0,1:T(8,128)(2,1)S(1)} fusion(bf16[1,4,256]{2,1,0:T(4,128)(2,1)S(1)} %collective-permute-done.1, bf16[1,2048,256]{2,1,0:T(8,128)(2,1)} %copy-done.6, bf16[1,4,256]{2,1,0:T(4,128)(2,1)} %copy-done.18), kind=kLoop, calls=%fused_computation.57 | loop fusion | flops 15728640 | bytes 4198400 | tf_op jit(solution)/shard_map/dot_general | solution.py:46
  37.8 3.0 %copy.14 = bf16[768,2048]{1,0:T(8,128)(2,1)} copy(bf16[768,2048]{0,1:T(8,128)(2,1)S(1)} %fusion.37) | data formatting | bytes 6291456 | tf_op jit(solution)/shard_map/dot_general | solution.py:46
  40.8 6.2 %convolution_bitcast_fusion.1 = f32[1,2048,512]{2,1,0:T(8,128)S(1)} fusion(bf16[1,16,256]{2,1,0:T(8,128)(2,1)S(1)} %collective-permute-done.3, bf16[1,2048,256]{2,1,0:T(8,128)(2,1)} %copy-done.4, bf16[1,16,256]{2,1,0:T(8,128)(2,1)} %collective-permute-done.2, bf16[768,256]{1,0:T(8,128)(2,1)} %bitcast.50, bf16[768,256]{1,0:T(8,128)(2,1)S(1)} %bitcast.48), kind=kOutput, calls=%fused_computation.1 | convolution fusion | flops 1627914240 | bytes 6045696 | tf_op jit(solution)/shard_map/dot_general | solution.py:40
  47.1 3.3 %fusion.28 = (bf16[1,2048,256]{2,1,0:T(8,128)(2,1)S(1)}, bf16[1,2048,256]{2,1,0:T(8,128)(2,1)}) fusion(bf16[1,2048,256]{2,1,0:T(8,128)(2,1)S(1)} %copy-done.12, f32[1,2048,512]{2,1,0:T(8,128)S(1)} %convolution_bitcast_fusion.1, f32[1,2048,512]{2,1,0:T(8,128)S(1)} %copy-done.2), kind=kLoop, calls=%fused_computation.43 | loop fusion | flops 18874368 | bytes 11534336 | tf_op jit(solution)/shard_map/convert_element_type | solution.py:91
  50.4 3.1 %collective-permute-start.5 = (bf16[1,16,256]{2,1,0:T(8,128)(2,1)S(1)}, bf16[1,16,256]{2,1,0:T(8,128)(2,1)S(1)}, u32[]{:S(2)}, u32[]{:S(2)}) collective-permute-start(bf16[1,16,256]{2,1,0:T(8,128)(2,1)S(1)} %get-tuple-element.8), channel_id=1, source_target_pairs={{0,1},{1,2},{2,3},{4,5},{5,6},{6,7},{8,9},{9,10},{10,11},{12,13},{... | collective-permute-start | bytes 24584 | tf_op jit(solution)/shard_map/ppermute | solution.py:18
  53.5 1.5 collective-permute-start.4
  55.0 7.9 %fusion.39 = bf16[768,2048]{0,1:T(8,128)(2,1)S(1)} fusion(bf16[1,16,256]{2,1,0:T(8,128)(2,1)S(1)} %collective-permute-done.3, bf16[1,2048,256]{2,1,0:T(8,128)(2,1)S(1)} %copy-done.5, bf16[1,16,256]{2,1,0:T(8,128)(2,1)} %collective-permute-done.2), kind=kLoop, calls=%fused_computation.58 | loop fusion | flops 15728640 | bytes 4210688 | tf_op jit(solution)/shard_map/dot_general | solution.py:46
  62.8 3.0 %copy.17 = bf16[768,2048]{1,0:T(8,128)(2,1)} copy(bf16[768,2048]{0,1:T(8,128)(2,1)S(1)} %fusion.39) | data formatting | bytes 6291456 | tf_op jit(solution)/shard_map/dot_general | solution.py:46
  65.8 3.2 %fusion.32 = f32[3,256,256]{2,1,0:T(8,128)S(1)} fusion(bf16[3,256,2048]{2,1,0:T(8,128)(2,1)} %bitcast.47, bf16[1,2048,256]{2,1,0:T(8,128)(2,1)} %copy-done.10), kind=kOutput, calls=%fused_computation.52 | convolution fusion | flops 805306368 | bytes 4980736 | tf_op jit(solution)/shard_map/dot_general | solution.py:46
  69.0 1.1 rev.16
  71.2 1.8 convolution_bitcast_fusion
  74.5 2.2 fusion.34
  76.7 1.1 rev.15
  78.8 134.4 %all-reduce.3.cloned.1.call-done = (f32[3,256,256]{2,1,0:T(8,128)}, f32[3,256,256]{2,1,0:T(8,128)}) async-done(((f32[3,256,256]{2,1,0:T(8,128)}, f32[3,256,256]{2,1,0:T(8,128)}), (f32[3,256,256]{2,1,0:T(8,128)}, f32[3,256,256]{2,1,0:T(8,128)})) %all-reduce.3.cloned.1.call-update) | async-done | bytes 1572880 | tf_op jit(solution)/shard_map/psum | solution.py:100
  213.2 2.1 copy.20
  (54 shorter events, 8.4 us)
Async XLA Ops:
  7.2 11.5 %copy-start.8 = (bf16[3,256,256]{2,1,0:T(8,128)(2,1)S(1)}, bf16[3,256,256]{2,1,0:T(8,128)(2,1)}, u32[]{:S(2)}) copy-start(bf16[3,256,256]{2,1,0:T(8,128)(2,1)} %param.8) | copy-start | bytes 1179652
  7.2 12.5 %copy-start.15 = (bf16[3,256,256]{2,1,0:T(8,128)(2,1)S(1)}, bf16[3,256,256]{2,1,0:T(8,128)(2,1)}, u32[]{:S(2)}) copy-start(bf16[3,256,256]{2,1,0:T(8,128)(2,1)} %param.7) | copy-start | bytes 1179652
  7.2 206.0 %all-reduce.3.cloned.1.call-start = ((), (), s32[]{:S(2)}) async-start(), calls=%async_computation | async-start | bytes 3145728 | tf_op jit(solution)/shard_map/psum | solution.py:100
  9.0 14.7 %copy-start.6 = (bf16[1,2048,256]{2,1,0:T(8,128)(2,1)}, bf16[1,2048,256]{2,1,0:T(8,128)(2,1)S(1)}, u32[]{:S(2)}) copy-start(bf16[1,2048,256]{2,1,0:T(8,128)(2,1)S(1)} %fusion.14) | copy-start | bytes 3145732
  9.1 12.9 %collective-permute-start.1 = (bf16[1,4,256]{2,1,0:T(4,128)(2,1)S(1)}, bf16[1,4,256]{2,1,0:T(4,128)(2,1)S(1)}, u32[]{:S(2)}, u32[]{:S(2)}) collective-permute-start(bf16[1,4,256]{2,1,0:T(4,128)(2,1)S(1)} %get-tuple-element.12), channel_id=1, source_target_pairs={{1,0},{2,1},{3,2},{5,4},{6,5},{7,6},{9,8},{10,9},{11,10},{13,12},{... | collective-permute-start | bytes 6152 | tf_op jit(solution)/shard_map/ppermute | solution.py:20
  10.4 11.6 %collective-permute-start = (bf16[1,4,256]{2,1,0:T(4,128)(2,1)S(1)}, bf16[1,4,256]{2,1,0:T(4,128)(2,1)S(1)}, u32[]{:S(2)}, u32[]{:S(2)}) collective-permute-start(bf16[1,4,256]{2,1,0:T(4,128)(2,1)S(1)} %get-tuple-element.11), channel_id=1, source_target_pairs={{0,1},{1,2},{2,3},{4,5},{5,6},{6,7},{8,9},{9,10},{10,11},{12,13},{... | collective-permute-start | bytes 6152 | tf_op jit(solution)/shard_map/ppermute | solution.py:18
  18.7 5.1 %copy-start.9 = (bf16[3,256,256]{2,1,0:T(8,128)(2,1)}, bf16[3,256,256]{2,1,0:T(8,128)(2,1)S(1)}, u32[]{:S(2)}) copy-start(bf16[3,256,256]{2,1,0:T(8,128)(2,1)S(1)} %rev.14) | copy-start | bytes 1179652
  23.8 2.0 copy-start.1
  25.8 1.9 copy-start.4
  26.4 14.4 %collective-permute-start.3 = (bf16[1,16,256]{2,1,0:T(8,128)(2,1)}, bf16[1,16,256]{2,1,0:T(8,128)(2,1)S(1)}, u32[]{:S(2)}, u32[]{:S(2)}) collective-permute-start(bf16[1,16,256]{2,1,0:T(8,128)(2,1)} %get-tuple-element.10), channel_id=1, source_target_pairs={{1,0},{2,1},{3,2},{5,4},{6,5},{7,6},{9,8},{10,9},{11,10},{13,12},{... | collective-permute-start | bytes 24584 | tf_op jit(solution)/shard_map/ppermute | solution.py:20
  27.7 13.1 %collective-permute-start.2 = (bf16[1,16,256]{2,1,0:T(8,128)(2,1)}, bf16[1,16,256]{2,1,0:T(8,128)(2,1)}, u32[]{:S(2)}, u32[]{:S(2)}) collective-permute-start(bf16[1,16,256]{2,1,0:T(8,128)(2,1)} %get-tuple-element.9), channel_id=1, source_target_pairs={{0,1},{1,2},{2,3},{4,5},{5,6},{6,7},{8,9},{9,10},{10,11},{12,13},{... | collective-permute-start | bytes 24584 | tf_op jit(solution)/shard_map/ppermute | solution.py:18
  40.8 6.3 %copy-start.2 = (f32[1,2048,512]{2,1,0:T(8,128)S(1)}, f32[1,2048,512]{2,1,0:T(8,128)}, u32[]{:S(2)}) copy-start(f32[1,2048,512]{2,1,0:T(8,128)} %copy-done.1) | copy-start | bytes 12582916
  40.8 6.3 %copy-start.12 = (bf16[1,2048,256]{2,1,0:T(8,128)(2,1)S(1)}, bf16[1,2048,256]{2,1,0:T(8,128)(2,1)}, u32[]{:S(2)}) copy-start(bf16[1,2048,256]{2,1,0:T(8,128)(2,1)} %param.9) | copy-start | bytes 3145732
  47.1 7.9 %copy-start.5 = (bf16[1,2048,256]{2,1,0:T(8,128)(2,1)S(1)}, bf16[1,2048,256]{2,1,0:T(8,128)(2,1)}, u32[]{:S(2)}) copy-start(bf16[1,2048,256]{2,1,0:T(8,128)(2,1)} %copy-done.4) | copy-start | bytes 3145732
  50.4 3.1 %copy-start.10 = (bf16[1,2048,256]{2,1,0:T(8,128)(2,1)}, bf16[1,2048,256]{2,1,0:T(8,128)(2,1)S(1)}, u32[]{:S(2)}) copy-start(bf16[1,2048,256]{2,1,0:T(8,128)(2,1)S(1)} %get-tuple-element.5) | copy-start | bytes 3145732
  50.4 20.7 %collective-permute-start.5 = (bf16[1,16,256]{2,1,0:T(8,128)(2,1)S(1)}, bf16[1,16,256]{2,1,0:T(8,128)(2,1)S(1)}, u32[]{:S(2)}, u32[]{:S(2)}) collective-permute-start(bf16[1,16,256]{2,1,0:T(8,128)(2,1)S(1)} %get-tuple-element.8), channel_id=1, source_target_pairs={{0,1},{1,2},{2,3},{4,5},{5,6},{6,7},{8,9},{9,10},{10,11},{12,13},{... | collective-permute-start | bytes 24584 | tf_op jit(solution)/shard_map/ppermute | solution.py:18
  53.5 17.6 %collective-permute-start.4 = (bf16[1,16,256]{2,1,0:T(8,128)(2,1)S(1)}, bf16[1,16,256]{2,1,0:T(8,128)(2,1)S(1)}, u32[]{:S(2)}, u32[]{:S(2)}) collective-permute-start(bf16[1,16,256]{2,1,0:T(8,128)(2,1)S(1)} %get-tuple-element.7), channel_id=1, source_target_pairs={{1,0},{2,1},{3,2},{5,4},{6,5},{7,6},{9,8},{10,9},{11,10},{13,12},{... | collective-permute-start | bytes 24584 | tf_op jit(solution)/shard_map/ppermute | solution.py:20
  69.0 2.1 copy-start.11
  69.0 2.1 copy-start.16
  69.0 2.1 copy-start.17
  71.1 2.2 copy-start.3
  71.1 3.2 %copy-start.7 = (bf16[768,2048]{1,0:T(8,128)(2,1)S(1)}, bf16[768,2048]{1,0:T(8,128)(2,1)}, u32[]{:S(2)}) copy-start(bf16[768,2048]{1,0:T(8,128)(2,1)} %copy.14) | copy-start | bytes 9437188
  71.1 3.4 %copy-start.13 = (bf16[1,2048,256]{2,1,0:T(8,128)(2,1)S(1)}, bf16[1,2048,256]{2,1,0:T(8,128)(2,1)}, u32[]{:S(2)}) copy-start(bf16[1,2048,256]{2,1,0:T(8,128)(2,1)} %param.9) | copy-start | bytes 3145732
  213.2 2.1 copy-start.14
  (2 other events, 2.6 us)
Sparse Core Ops, SparseCore 0:
  78.9 134.1 all-reduce.2
where the time goes:
time: 224 us; the launch traced here: 223 us
  waiting for transfers between devices  134 us (60%)
  local copies, waits for them, and re-layouts  23.7 us (11%)
  other arithmetic  18.3 us (8%)
  matrix products  16.4 us (7%)
  starting transfers between devices  15.9 us (7%)
  between operations  14.4 us (6%)
    psum x1, waiting for transfers between devices, local(): first_weight_gradient = lax.psum(first_weight_gradient, ('dp', 'seq'))  134 us
    dot_general x2, other arithmetic, weight_term(): jnp.dot(stacked.reshape(-1, 3 * channels).T, grad.reshape(-1, channels),...  12.2 us
    ppermute x3, starting transfers between devices, with_halo(): lax.ppermute(tail, axis, [(i, (i + 1) % count) for i in range(ends)])  11.8 us
    dot_general x4, matrix products, product(): jnp.dot(stacked.reshape(-1, shape_in[-1]), matrix, preferred_element_type...  11.1 us
    unnamed x41, local copies, waits for them, and re-layouts  7.38 us
    rev x2, local copies, waits for them, and re-layouts, layer_forward_pass(): reversed_taps = weight[::-1, ::-1, ::-1].reshape(-1, channels)  6.64 us
    dot_general x2, local copies, waits for them, and re-layouts, weight_term(): jnp.dot(stacked.reshape(-1, 3 * channels).T, grad.reshape(-1, channels),...  5.97 us
    dot_general x2, matrix products, weight_term(): jnp.dot(stacked.reshape(-1, 3 * channels).T, grad.reshape(-1, channels),...  5.36 us
  transfers between devices with their start and end apart: 7, of which 1 were waited for; matrix products, arithmetic and copies ran while one was open for 14% of the time, Pallas kernels for 0%

commit v1 on v0

v1 whole, which is shorter than its diff:
```python
import functools

import jax
import jax.numpy as jnp
from jax import lax
from jax.experimental import pallas as pl
from jax.experimental.pallas import tpu as pltpu
from jax.sharding import PartitionSpec as P

FIRST_DILATION = 4
SECOND_DILATION = 16
LANES = 128
TILE = 256
BASES = 4
NONE = 4
BF16 = jnp.bfloat16
F32 = jnp.float32
MESH = pl.DeviceIdType.MESH
VMEM = pl.BlockSpec(memory_space=pltpu.VMEM)
ANY = pl.BlockSpec(memory_space=pl.ANY)
GELU_A = 0.7978845608028654
GELU_B = 0.044715


def dot(a, b):
    return jnp.dot(a, b, preferred_element_type=F32)


def dot_rows(a, b):
    return lax.dot_general(a, b, (((0,), (0,)), ((), ())), preferred_element_type=F32)


def flip_matrix(n):
    row = lax.broadcasted_iota(jnp.int32, (n, n), 0)
    col = lax.broadcasted_iota(jnp.int32, (n, n), 1)
    return (row + col == n - 1).astype(F32).astype(BF16)


def gelu_pair(x):
    square = x * x
    t = jnp.tanh(x * (GELU_A + (GELU_A * GELU_B) * square))
    half = 0.5 + 0.5 * t
    slope = GELU_A + (3.0 * GELU_A * GELU_B) * square
    return x * half, half + (0.5 * x) * (1.0 - t * t) * slope


def halo_kernel(count, codes_ref, cot_ref, ext_ref, halo_ref, code_in, cot_in, send, recv):
    me = lax.axis_index("seq")
    right, left = lax.rem(me + 1, count), lax.rem(me + count - 1, count)
    barrier = pltpu.get_barrier_semaphore()
    for peer in (left, right):
        pl.semaphore_signal(barrier, inc=1, device_id={"seq": peer}, device_id_type=MESH)
    pl.semaphore_wait(barrier, 2)
    length = codes_ref.shape[1]
    wide = SECOND_DILATION
    copies = []
    for i, (src, dst, peer) in enumerate(
        (
            (codes_ref.at[:, pl.ds(length - LANES, LANES)], code_in.at[0], right),
            (codes_ref.at[:, pl.ds(0, LANES)], code_in.at[1], left),
            (cot_ref.at[0, pl.ds(length - wide, wide)], cot_in.at[0], right),
            (cot_ref.at[0, pl.ds(0, wide)], cot_in.at[1], left),
        )
    ):
        copy = pltpu.make_async_remote_copy(
            src_ref=src,
            dst_ref=dst,
            send_sem=send.at[i],
            recv_sem=recv.at[i],
            device_id={"seq": peer},
            device_id_type=MESH,
        )
        copy.start()
        copies.append(copy)
    ext_ref[:, LANES : LANES + length] = codes_ref[...]
    for copy in copies:
        copy.wait()
    first, last = me == 0, me == count - 1
    ext_ref[:, :LANES] = jnp.where(first, NONE, code_in[0])
    ext_ref[:, LANES + length :] = jnp.where(last, NONE, code_in[1])
    zero = jnp.zeros((), BF16)
    halo_ref[:wide] = jnp.where(first, zero, cot_in[0])
    halo_ref[wide:] = jnp.where(last, zero, cot_in[1])


def exchange_halos(codes, cot):
    length, channels = cot.shape[1:]
    return pl.pallas_call(
        functools.partial(halo_kernel, lax.axis_size("seq")),
        out_shape=(
            jax.ShapeDtypeStruct((1, length + 2 * LANES), jnp.int32),
            jax.ShapeDtypeStruct((2 * SECOND_DILATION, channels), BF16),
        ),
        in_specs=[VMEM, ANY],
        out_specs=(VMEM, VMEM),
        scratch_shapes=[
            pltpu.VMEM((2, 1, LANES), jnp.int32),
            pltpu.VMEM((2, SECOND_DILATION, channels), BF16),
            pltpu.SemaphoreType.DMA((4,)),
            pltpu.SemaphoreType.DMA((4,)),
        ],
        compiler_params=pltpu.CompilerParams(collective_id=0, has_side_effects=True),
        name="halos",
    )(codes, cot)


def panel_kernel(
    ext_ref, halo_ref, cot_ref, embed_ref, first_ref, second_ref,
    block_ref, sums_ref,
    onehot, hidden, slope_one, grad_two, weight, weight_t, total,
):
    length, channels = cot_ref.shape[1:]
    wide = SECOND_DILATION
    span = ext_ref.shape[1]
    flip = flip_matrix(channels)

    def flipped(x):
        return dot(dot(flip, x).astype(BF16), flip)

    embed = embed_ref[...]
    table = jnp.zeros((16, channels), F32)
    for k in range(3):
        pair = second_ref[k].astype(F32) + flipped(second_ref[2 - k])
        weight[k] = pair.astype(BF16)
        weight_t[k] = pair.T.astype(BF16)
        row = lax.broadcasted_iota(jnp.int32, (16, BASES), 0)
        col = lax.broadcasted_iota(jnp.int32, (16, BASES), 1)
        place = (row == BASES * k + col).astype(F32).astype(BF16)
        rows = dot(place, embed).astype(BF16)
        table = table + dot(rows, first_ref[k])
        table = table + dot(rows, flipped(first_ref[2 - k]).astype(BF16))
    high = table.astype(BF16)
    rest = table - high.astype(F32)
    middle = rest.astype(BF16)
    low = (rest - middle.astype(F32)).astype(BF16)
    table = jnp.concatenate([high, middle, low], axis=0)

    codes = jnp.broadcast_to(ext_ref[...], (16, span))
    row = lax.broadcasted_iota(jnp.int32, (16, span), 0)
    before = pltpu.roll(codes, FIRST_DILATION, 1)
    after = pltpu.roll(codes, span - FIRST_DILATION, 1)
    tap = row // BASES
    seen = jnp.where(tap == 0, before, jnp.where(tap == 1, codes, after))
    hit = (seen == row % BASES) & (codes < NONE) & (row < 3 * BASES)
    hit = hit.astype(F32).astype(BF16)
    for part in range(3):
        onehot[16 * part : 16 * part + 16] = hit

    for start in range(0, span, TILE):
        size = min(TILE, span - start)
        pre = dot_rows(onehot[:, start : start + size], table)
        value, slope = gelu_pair(pre)
        hidden[start : start + size] = value.astype(BF16)
        slope_one[start : start + size] = slope

    def layer_two(start, size, cot):
        at = LANES + start
        pre = dot(hidden[at - wide : at - wide + size], weight[0])
        pre = pre + dot(hidden[at : at + size], weight[1])
        pre = pre + dot(hidden[at + wide : at + wide + size], weight[2])
        value, slope = gelu_pair(pre)
        grad_two[start + wide : start + wide + size] = (cot.astype(F32) * slope).astype(BF16)
        return value

    layer_two(-wide, wide, halo_ref[:wide])
    layer_two(length, wide, halo_ref[wide:])
    for start in range(0, length, TILE):
        value = layer_two(start, TILE, cot_ref[0, start : start + TILE])
        value = hidden[LANES + start : LANES + start + TILE].astype(F32) + value
        block_ref[0, start : start + TILE] = value.astype(BF16)

    sums = jnp.zeros((16, channels), F32)
    for start in range(0, length, TILE):
        at = LANES + start
        ahead, here, behind = (
            grad_two[start + shift : start + shift + TILE] for shift in (2 * wide, wide, 0)
        )
        value = hidden[at : at + TILE].T
        for k, grad in enumerate((ahead, here, behind)):
            term = dot(value, grad)
            total[k] = term if start == 0 else total[k] + term
        back = dot(ahead, weight_t[0]) + dot(here, weight_t[1]) + dot(behind, weight_t[2])
        back = back + cot_ref[0, start : start + TILE].astype(F32)
        grad_one = (back * slope_one[at : at + TILE]).astype(BF16)
        sums = sums + dot(onehot[:16, at : at + TILE], grad_one)

    def flipped_wide(x, rows):
        high = x.astype(BF16)
        low = (x - high.astype(F32)).astype(BF16)
        left = flip[:rows]
        return dot(dot(left, high).astype(BF16), flip) + dot(dot(left, low).astype(BF16), flip)

    half = channels // 2
    sums_ref[:channels] = (total[0] + flipped_wide(total[2], channels)).astype(BF16)
    sums_ref[channels : channels + half] = (total[1, :half] + flipped_wide(total[1], half)).astype(BF16)
    sums_ref[channels + half : channels + half + 16] = sums.astype(BF16)
    left_over = sums_ref.shape[0] - (channels + half + 16)
    if left_over:
        sums_ref[channels + half + 16 :] = jnp.zeros((left_over, channels), BF16)


def panel(ext, halo, cot, embed, first, second, rows):
    length, channels = cot.shape[1:]
    span = ext.shape[1]
    return pl.pallas_call(
        panel_kernel,
        out_shape=(
            jax.ShapeDtypeStruct(cot.shape, BF16),
            jax.ShapeDtypeStruct((rows, channels), BF16),
        ),
        in_specs=[VMEM] * 6,
        out_specs=(VMEM, VMEM),
        scratch_shapes=[
            pltpu.VMEM((48, span), BF16),
            pltpu.VMEM((span, channels), BF16),
            pltpu.VMEM((span, channels), F32),
            pltpu.VMEM((length + 2 * SECOND_DILATION, channels), BF16),
            pltpu.VMEM((3, channels, channels), BF16),
            pltpu.VMEM((3, channels, channels), BF16),
            pltpu.VMEM((3, channels, channels), F32),
        ],
        compiler_params=pltpu.CompilerParams(vmem_limit_bytes=40 * 1024 * 1024),
        name="panel",
    )(ext, halo, cot, embed, first, second)


def reduce_kernel(across, along, x_ref, o_ref, in_seq, part, in_dp, held, *sems):
    d, q = lax.axis_index("dp"), lax.axis_index("seq")
    barrier = pltpu.get_barrier_semaphore()
    seq_peers = [lax.rem(q + o, along) for o in range(1, along)]
    dp_peers = [lax.rem(d + o, across) for o in range(1, across)]
    for peer in seq_peers:
        pl.semaphore_signal(barrier, inc=1, device_id={"seq": peer}, device_id_type=MESH)
    for peer in dp_peers:
        pl.semaphore_signal(barrier, inc=1, device_id={"dp": peer}, device_id_type=MESH)
    pl.semaphore_wait(barrier, along + across - 2)

    def start(axis, phase, i, peer, src, dst):
        copy = pltpu.make_async_remote_copy(
            src_ref=src,
            dst_ref=dst,
            send_sem=sems[2 * phase].at[i],
            recv_sem=sems[2 * phase + 1].at[i],
            device_id={axis: peer},
            device_id_type=MESH,
        )
        copy.start()
        return copy

    def wait_all(copies):
        for copy in copies:
            copy.wait_recv()
        for copy in copies:
            copy.wait_send()

    copies = [
        start("seq", 0, i, peer, x_ref.at[peer], in_seq.at[i]) for i, peer in enumerate(seq_peers)
    ]
    wait_all(copies)
    value = x_ref[q].astype(F32)
    for i in range(along - 1):
        value = value + in_seq[i].astype(F32)
    part[...] = value.astype(BF16)

    copies = [start("dp", 1, i, peer, part.at[peer], in_dp.at[i]) for i, peer in enumerate(dp_peers)]
    wait_all(copies)
    value = part[d].astype(F32)
    for i in range(across - 1):
        value = value + in_dp[i].astype(F32)
    held[q, d] = value.astype(BF16)

    mine = held.at[q, d]
    copies = [start("dp", 2, i, peer, mine, mine) for i, peer in enumerate(dp_peers)]
    wait_all(copies)
    mine = held.at[q]
    copies = [start("seq", 3, i, peer, mine, mine) for i, peer in enumerate(seq_peers)]
    wait_all(copies)
    o_ref[...] = held[...]


def reduce_sums(x):
    along, across, rows, channels = x.shape
    sems = []
    for count in (along, across, across, along):
        sems += [pltpu.SemaphoreType.DMA((count - 1,))] * 2
    return pl.pallas_call(
        functools.partial(reduce_kernel, across, along),
        out_shape=jax.ShapeDtypeStruct(x.shape, BF16),
        in_specs=[VMEM],
        out_specs=VMEM,
        scratch_shapes=[
            pltpu.VMEM((along - 1, across, rows, channels), BF16),
            pltpu.VMEM((across, rows, channels), BF16),
            pltpu.VMEM((across - 1, rows, channels), BF16),
            pltpu.VMEM(x.shape, BF16),
            *sems,
        ],
        compiler_params=pltpu.CompilerParams(
            collective_id=1, has_side_effects=True, vmem_limit_bytes=40 * 1024 * 1024
        ),
        name="sums",
    )(x)


def expand_kernel(x_ref, embed_ref, first_ref, second_ref):
    channels = embed_ref.shape[1]
    half = channels // 2
    flip = flip_matrix(channels)
    outer = x_ref[:channels]
    second_ref[0] = outer.astype(F32)
    second_ref[2] = dot(dot(flip, outer).astype(BF16), flip)
    inner = x_ref[channels : channels + half]
    second_ref[1, :half] = inner.astype(F32)
    second_ref[1, half:] = dot(dot(flip[half:, :half], inner).astype(BF16), flip)
    sums = x_ref[channels + half : channels + half + 16]
    sums_flip = dot(sums, flip).astype(BF16)
    embed = embed_ref[...]
    for k in range(3):
        row = lax.broadcasted_iota(jnp.int32, (16, BASES), 0)
        col = lax.broadcasted_iota(jnp.int32, (16, BASES), 1)
        here = dot((row == BASES * k + col).astype(F32).astype(BF16), embed).astype(BF16)
        there = dot((row == BASES * (2 - k) + col).astype(F32).astype(BF16), embed).astype(BF16)
        there = dot(there, flip).astype(BF16)
        first_ref[k] = dot_rows(here, sums) + dot_rows(there, sums_flip)


def expand(x, embed):
    channels = x.shape[1]
    shape = jax.ShapeDtypeStruct((3, channels, channels), F32)
    return pl.pallas_call(
        expand_kernel,
        out_shape=(shape, shape),
        in_specs=[VMEM] * 2,
        out_specs=(VMEM, VMEM),
        compiler_params=pltpu.CompilerParams(vmem_limit_bytes=32 * 1024 * 1024),
        name="expand",
    )(x, embed)


def local(codes, embed, first, second, cot):
    channels = cot.shape[2]
    across, along = lax.axis_size("dp"), lax.axis_size("seq")
    devices = across * along
    needed = channels + channels // 2 + 16
    rows = 16 * pl.cdiv(needed, 16 * devices)
    ext, halo = exchange_halos(codes, cot)
    block_out, sums = panel(ext, halo, cot, embed, first, second, rows * devices)
    sums = reduce_sums(sums.reshape(along, across, rows, channels))
    first_grad, second_grad = expand(sums.reshape(rows * devices, channels), embed)
    return block_out, first_grad, second_grad


def solution(mesh):
    in_specs = (P("dp", "seq"), P(), P(), P(), P("dp", "seq", None))
    out_specs = (P("dp", "seq", None), P(), P())
    return jax.shard_map(local, mesh=mesh, in_specs=in_specs, out_specs=out_specs, check_vma=False)
```

time: 224 us -> 40.8 us (0.18)
  waiting for transfers between devices: 134 us -> 0 us
  Pallas kernels: 0 us -> 35.6 us
  local copies, waits for them, and re-layouts: 23.7 us -> 4.08 us
  other arithmetic: 18.3 us -> 0 us
  matrix products: 16.4 us -> 0 us
  starting transfers between devices: 15.9 us -> 0 us
  between operations: 14.4 us -> 0.68 us
    psum x1 -> x0, waiting for transfers between devices: 134 us -> none  [local(): first_weight_gradient = lax.psum(first_weight_gradient, ('dp', 'seq'))]
    pallas_call x0 -> x4, Pallas kernels: none -> 35.6 us  [the longest x1 21 us: reduce_sums(): pl.pallas_call(functools.partial(reduce_kernel, across, along), out_shape...]
    dot_general x6 -> x0, matrix products: 16.4 us -> none  [the longest x4 11.1 us: product(): jnp.dot(stacked.reshape(-1, shape_in[-1]), matrix, preferred_element_type...]
    ppermute x6 -> x0, starting transfers between devices: 15.9 us -> none  [the longest x3 11.8 us: with_halo(): lax.ppermute(tail, axis, [(i, (i + 1) % count) for i in range(ends)])]
    dot_general x2 -> x0, other arithmetic: 12.2 us -> none  [weight_term(): jnp.dot(stacked.reshape(-1, 3 * channels).T, grad.reshape(-1, channels),...]
    rev x4 -> x0, local copies, waits for them, and re-layouts: 8.8 us -> none  [the longest x2 6.64 us: layer_forward_pass(): reversed_taps = weight[::-1, ::-1, ::-1].reshape(-1, channels)]
    dot_general x2 -> x0, local copies, waits for them, and re-layouts: 5.97 us -> none  [weight_term(): jnp.dot(stacked.reshape(-1, 3 * channels).T, grad.reshape(-1, channels),...]
    convert_element_type x2 -> x0, other arithmetic: 4.03 us -> none  [the longest x1 3.28 us: local(): back_two(cotangent_wide_float)[0].astype(jnp.bfloat16)]
  transfers between devices with their start and end apart: 7 -> 0, of which waited for: 1 -> 0; matrix products, arithmetic and copies ran while one was open for 14% -> 0% of each run, Pallas kernels for 0% -> 0%
where the time goes in v1:
time: 40.8 us; the launch traced here: 40.4 us
  Pallas kernels  35.6 us (87%)
  local copies, waits for them, and re-layouts  4.08 us (10%)
  between operations  0.68 us (2%)
    pallas_call x1, Pallas kernels, reduce_sums(): pl.pallas_call(functools.partial(reduce_kernel, across, along), out_shape...  21 us
    pallas_call x1, Pallas kernels, panel(): pl.pallas_call(panel_kernel, out_shape=(jax.ShapeDtypeStruct(cot.shape, B...  6.58 us
    pallas_call x1, Pallas kernels, exchange_halos(): pl.pallas_call(functools.partial(halo_kernel, lax.axis_size('seq')), out_...  6.1 us
    unnamed x12, local copies, waits for them, and re-layouts  4.08 us
    pallas_call x1, Pallas kernels, expand(): pl.pallas_call(expand_kernel, out_shape=(shape, shape), in_specs=[VMEM] *...  1.92 us

profile of v1, /device:TPU:0, one launch (start us, length us, event | category | flops | bytes accessed | tf_op | source)
XLA Modules:
  0.0 40.4 jit_solution(14872038063566237921)
XLA Ops:
  0.6 0.0 copy-start
  0.6 6.1 %halos.1 = (s32[1,2304]{1,0:T(1,128)}, bf16[32,256]{1,0:T(8,128)(2,1)}) custom-call(s32[1,2048]{1,0:T(1,128)} %codes_ref.1, bf16[1,2048,256]{2,1,0:T(8,128)(2,1)} %cot_ref.3), custom_call_target="tpu_custom_call" | custom-call | tf_op jit(solution)/shard_map/halos/pallas_call | solution.py:88
  6.8 0.0 copy-start.5
  6.8 0.0 copy-done
  6.8 0.7 %copy-done.5 = bf16[4,256]{1,0:T(4,128)(2,1)S(1)} copy-done((bf16[4,256]{1,0:T(4,128)(2,1)S(1)}, bf16[4,256]{1,0:T(4,128)(2,1)}, u32[]{:S(2)}) %copy-start.5) | copy-done | bytes 2072
  7.4 0.0 copy-start.1
  7.4 1.0 %copy-done.1 = bf16[3,256,256]{2,1,0:T(8,128)(2,1)S(1)} copy-done((bf16[3,256,256]{2,1,0:T(8,128)(2,1)S(1)}, bf16[3,256,256]{2,1,0:T(8,128)(2,1)}, u32[]{:S(2)}) %copy-start.1) | copy-done | bytes 393240
  8.4 0.0 copy-start.2
  8.4 1.0 %copy-done.2 = bf16[3,256,256]{2,1,0:T(8,128)(2,1)S(1)} copy-done((bf16[3,256,256]{2,1,0:T(8,128)(2,1)S(1)}, bf16[3,256,256]{2,1,0:T(8,128)(2,1)}, u32[]{:S(2)}) %copy-start.2) | copy-done | bytes 393240
  9.4 0.0 copy-start.3
  9.4 0.7 %copy-done.3 = bf16[32,256]{1,0:T(8,128)(2,1)S(1)} copy-done((bf16[32,256]{1,0:T(8,128)(2,1)S(1)}, bf16[32,256]{1,0:T(8,128)(2,1)}, u32[]{:S(2)}) %copy-start.3) | copy-done | bytes 16408
  10.1 0.0 copy-start.4
  10.2 0.7 %copy-done.4 = s32[1,2304]{1,0:T(1,128)S(1)} copy-done((s32[1,2304]{1,0:T(1,128)S(1)}, s32[1,2304]{1,0:T(1,128)}, u32[]{:S(2)}) %copy-start.4) | copy-done | bytes 9240
  10.8 6.6 %panel.1 = (bf16[1,2048,256]{2,1,0:T(8,128)(2,1)}, bf16[512,256]{1,0:T(8,128)(2,1)S(1)}) custom-call(s32[1,2304]{1,0:T(1,128)S(1)} %copy-done.4, bf16[32,256]{1,0:T(8,128)(2,1)S(1)} %copy-done.3, bf16[1,2048,256]{2,1,0:T(8,128)(2,1)S(1)} %copy-done, bf16[4,256]{1,0:T(4,128)(2,1)S(1)} %copy-done.5, bf16[3,256,256]{2,1,0:T(8,128)(2,1)S(1)} %copy-done.1, ...), custom_call_target="tpu_custom_call" | custom-call | tf_op jit(solution)/shard_map/panel/pallas_call | solution.py:205
  17.4 21.0 %sums.1 = bf16[4,8,16,256]{3,2,1,0:T(8,128)(2,1)S(1)} custom-call(bf16[4,8,16,256]{3,2,1,0:T(8,128)(2,1)S(1)} %bitcast.3), custom_call_target="tpu_custom_call" | custom-call | tf_op jit(solution)/shard_map/sums/pallas_call | solution.py:286
  38.5 1.9 %expand.1 = (f32[3,256,256]{2,1,0:T(8,128)}, f32[3,256,256]{2,1,0:T(8,128)}) custom-call(bf16[512,256]{1,0:T(8,128)(2,1)S(1)} %bitcast.2, bf16[4,256]{1,0:T(4,128)(2,1)S(1)} %copy-done.5), custom_call_target="tpu_custom_call" | custom-call | tf_op jit(solution)/shard_map/expand/pallas_call | solution.py:330
Async XLA Ops:
  0.6 6.1 %copy-start = (bf16[1,2048,256]{2,1,0:T(8,128)(2,1)S(1)}, bf16[1,2048,256]{2,1,0:T(8,128)(2,1)}, u32[]{:S(2)}) copy-start(bf16[1,2048,256]{2,1,0:T(8,128)(2,1)} %cot_ref.3) | copy-start | bytes 3145732
  6.8 0.7 %copy-start.5 = (bf16[4,256]{1,0:T(4,128)(2,1)S(1)}, bf16[4,256]{1,0:T(4,128)(2,1)}, u32[]{:S(2)}) copy-start(bf16[4,256]{1,0:T(4,128)(2,1)} %embed_ref.3) | copy-start | bytes 6148
  7.4 1.0 %copy-start.1 = (bf16[3,256,256]{2,1,0:T(8,128)(2,1)S(1)}, bf16[3,256,256]{2,1,0:T(8,128)(2,1)}, u32[]{:S(2)}) copy-start(bf16[3,256,256]{2,1,0:T(8,128)(2,1)} %first_ref.1) | copy-start | bytes 1179652
  8.4 1.0 %copy-start.2 = (bf16[3,256,256]{2,1,0:T(8,128)(2,1)S(1)}, bf16[3,256,256]{2,1,0:T(8,128)(2,1)}, u32[]{:S(2)}) copy-start(bf16[3,256,256]{2,1,0:T(8,128)(2,1)} %second_ref.1) | copy-start | bytes 1179652
  9.4 0.7 %copy-start.3 = (bf16[32,256]{1,0:T(8,128)(2,1)S(1)}, bf16[32,256]{1,0:T(8,128)(2,1)}, u32[]{:S(2)}) copy-start(bf16[32,256]{1,0:T(8,128)(2,1)} %get-tuple-element.10.halo_ref) | copy-start | bytes 49156
  10.1 0.7 %copy-start.4 = (s32[1,2304]{1,0:T(1,128)S(1)}, s32[1,2304]{1,0:T(1,128)}, u32[]{:S(2)}) copy-start(s32[1,2304]{1,0:T(1,128)} %get-tuple-element.9.ext_ref) | copy-start | bytes 27652

commit v2 on v0

v2 whole, which is shorter than its diff:
```python
import functools

import jax
import jax.numpy as jnp
from jax import lax
from jax.experimental import pallas as pl
from jax.experimental.pallas import tpu as pltpu
from jax.sharding import PartitionSpec as P

FIRST_DILATION = 4
SECOND_DILATION = 16
LANES = 128
TILE = 256
BASES = 4
NONE = 4
BF16 = jnp.bfloat16
F32 = jnp.float32
MESH = pl.DeviceIdType.MESH
UNROLL = 8
VMEM = pl.BlockSpec(memory_space=pltpu.VMEM)
ANY = pl.BlockSpec(memory_space=pl.ANY)
GELU_A = 0.7978845608028654
GELU_B = 0.044715


def dot(a, b):
    return jnp.dot(a, b, preferred_element_type=F32)


def dot_rows(a, b):
    return lax.dot_general(a, b, (((0,), (0,)), ((), ())), preferred_element_type=F32)


def flip_matrix(n):
    row = lax.broadcasted_iota(jnp.int32, (n, n), 0)
    col = lax.broadcasted_iota(jnp.int32, (n, n), 1)
    return (row + col == n - 1).astype(F32).astype(BF16)


def gelu_pair(x):
    square = x * x
    t = jnp.tanh(x * (GELU_A + (GELU_A * GELU_B) * square))
    half = 0.5 + 0.5 * t
    slope = GELU_A + (3.0 * GELU_A * GELU_B) * square
    return x * half, half + (0.5 * x) * (1.0 - t * t) * slope


def panel_kernel(
    across, along, blocks,
    codes_ref, cot_ref, embed_ref, first_ref, second_ref,
    block_ref, rows_ref, sums_ref,
    ext, cot, first, second, code_in, cot_in, onehot, hidden, slope_one, grad_two,
    weight, weight_t, total, acc, mine, own_sum, in_seq, in_sum, part, in_dp, held, block,
    load, halo_send, halo_recv, *sems,
):
    d, q = lax.axis_index("dp"), lax.axis_index("seq")
    seq_peers = [lax.rem(q + o, along) for o in range(1, along)]
    dp_peers = [lax.rem(d + o, across) for o in range(1, across)]
    right, left = seq_peers[0], seq_peers[-1]
    length, channels = cot_ref.shape[1:]
    half = channels // 2
    wide = SECOND_DILATION
    span = ext.shape[1]
    tiles = length // TILE

    loads = [
        pltpu.make_async_copy(src, dst, load.at[i])
        for i, (src, dst) in enumerate(
            (
                (second_ref, second),
                (first_ref, first),
                (codes_ref, ext.at[:, pl.ds(LANES, length)]),
                (cot_ref, cot),
            )
        )
    ]
    for copy in loads:
        copy.start()

    barrier = pltpu.get_barrier_semaphore()
    for peer in seq_peers:
        pl.semaphore_signal(barrier, inc=1, device_id={"seq": peer}, device_id_type=MESH)
    for peer in dp_peers:
        pl.semaphore_signal(barrier, inc=1, device_id={"dp": peer}, device_id_type=MESH)

    def send(axis, peer, src, dst, send_sem, recv_sem):
        copy = pltpu.make_async_remote_copy(
            src_ref=src,
            dst_ref=dst,
            send_sem=send_sem,
            recv_sem=recv_sem,
            device_id={axis: peer},
            device_id_type=MESH,
        )
        copy.start()
        return copy

    def send_all(axis, peers, phase, src, dst):
        out, into = sems[2 * phase], sems[2 * phase + 1]
        return [
            send(axis, peer, src(peer), dst(i), out.at[i], into.at[i])
            for i, peer in enumerate(peers)
        ]

    flip = flip_matrix(channels)

    def flipped(x):
        return dot(dot(flip, x).astype(BF16), flip)

    embed = embed_ref[...]
    loads[0].wait()
    for k in range(3):
        pair = second[k].astype(F32) + flipped(second[2 - k])
        weight[k] = pair.astype(BF16)
        weight_t[k] = pair.T.astype(BF16)
    loads[1].wait()
    table = jnp.zeros((16, channels), F32)
    for k in range(3):
        row = lax.broadcasted_iota(jnp.int32, (16, BASES), 0)
        col = lax.broadcasted_iota(jnp.int32, (16, BASES), 1)
        place = (row == BASES * k + col).astype(F32).astype(BF16)
        rows = dot(place, embed).astype(BF16)
        table = table + dot(rows, first[k])
        table = table + dot(rows, flipped(first[2 - k]).astype(BF16))
    high = table.astype(BF16)
    rest = table - high.astype(F32)
    middle = rest.astype(BF16)
    low = (rest - middle.astype(F32)).astype(BF16)
    table = jnp.concatenate([high, middle, low], axis=0)

    pl.semaphore_wait(barrier, along + across - 2)
    halos = [
        send(axis, peer, src, dst, halo_send.at[i], halo_recv.at[i])
        for i, (axis, peer, src, dst) in enumerate(
            (
                ("seq", right, codes_ref.at[:, pl.ds(length - LANES, LANES)], code_in.at[0]),
                ("seq", left, codes_ref.at[:, pl.ds(0, LANES)], code_in.at[1]),
                ("seq", right, cot_ref.at[0, pl.ds(length - wide, wide)], cot_in.at[0]),
                ("seq", left, cot_ref.at[0, pl.ds(0, wide)], cot_in.at[1]),
            )
        )
    ]

    def fill_onehot():
        codes = jnp.broadcast_to(ext[...], (16, span))
        row = lax.broadcasted_iota(jnp.int32, (16, span), 0)
        before = pltpu.roll(codes, FIRST_DILATION, 1)
        after = pltpu.roll(codes, span - FIRST_DILATION, 1)
        tap = row // BASES
        seen = jnp.where(tap == 0, before, jnp.where(tap == 1, codes, after))
        hit = (seen == row % BASES) & (codes < NONE) & (row < 3 * BASES)
        hit = hit.astype(F32).astype(BF16)
        for copy in range(3):
            onehot[16 * copy : 16 * copy + 16] = hit

    def at(start, size):
        return pl.ds(pl.multiple_of(start, wide), size)

    def layer_one(start, size):
        place = pl.ds(pl.multiple_of(start, LANES), size)
        value, slope = gelu_pair(dot_rows(onehot[:, place], table))
        hidden[place] = value.astype(BF16)
        slope_one[place] = slope

    def layer_two(start, size, grad):
        pre = dot(hidden[at(start + LANES - wide, size)], weight[0])
        pre = pre + dot(hidden[at(start + LANES, size)], weight[1])
        pre = pre + dot(hidden[at(start + LANES + wide, size)], weight[2])
        value, slope = gelu_pair(pre)
        grad_two[at(start + wide, size)] = (grad.astype(F32) * slope).astype(BF16)
        return value

    def tile_one(i):
        layer_one(i * TILE + LANES, TILE)

    def tile_two(i):
        start = i * TILE
        value = layer_two(start, TILE, cot[0, at(start, TILE)])
        value = hidden[at(start + LANES, TILE)].astype(F32) + value
        block[0, at(start, TILE)] = value.astype(BF16)

    def loop(first, last, body):
        if last > first:
            lax.fori_loop(first, last, lambda i, c: (body(i), c)[1], 0, unroll=min(UNROLL, last - first))

    ext[:, :LANES] = jnp.full((1, LANES), NONE, jnp.int32)
    ext[:, LANES + length :] = jnp.full((1, LANES), NONE, jnp.int32)
    loads[2].wait()
    fill_onehot()
    loop(1, tiles - 1, tile_one)
    loads[3].wait()
    loop(2, tiles - 2, tile_two)

    for copy in halos:
        copy.wait()
    at_first, at_last = q == 0, q == along - 1
    ext[:, :LANES] = jnp.where(at_first, NONE, code_in[0])
    ext[:, LANES + length :] = jnp.where(at_last, NONE, code_in[1])
    fill_onehot()
    layer_one(0, LANES + TILE)
    layer_one(span - LANES - TILE, LANES + TILE)
    zero = jnp.zeros((), BF16)
    layer_two(-wide, wide, jnp.where(at_first, zero, cot_in[0]))
    layer_two(length, wide, jnp.where(at_last, zero, cot_in[1]))
    for i in (0, 1, tiles - 2, tiles - 1):
        tile_two(i)

    stored = pltpu.make_async_copy(block, block_ref, load.at[4])
    stored.start()

    total[...] = jnp.zeros_like(total)

    def tile_terms(i):
        start = i * TILE
        value = hidden[at(start + LANES, TILE)].T
        for k in range(3):
            total[k] += dot(value, grad_two[at(start + (2 - k) * wide, TILE)])

    loop(0, tiles, tile_terms)

    def flipped_wide(x, rows):
        high = x.astype(BF16)
        low = (x - high.astype(F32)).astype(BF16)
        left = flip[:rows]
        return dot(dot(left, high).astype(BF16), flip) + dot(dot(left, low).astype(BF16), flip)

    outer = (total[0] + flipped_wide(total[2], channels)).astype(BF16)
    inner = (total[1, :half] + flipped_wide(total[1], half)).astype(BF16)
    filled = (channels + half) // 16
    for b in range(along * blocks):
        if 16 * b < channels:
            value = outer[16 * b : 16 * b + 16]
        elif b < filled:
            value = inner[16 * b - channels : 16 * b - channels + 16]
        else:
            value = jnp.zeros((16, channels), BF16)
        mine[b // blocks, b % blocks] = value

    first_copies = send_all("seq", seq_peers, 0, lambda peer: mine.at[peer], lambda i: in_seq.at[i])

    acc[...] = jnp.zeros_like(acc)

    def tile_back(i):
        start = i * TILE
        back = cot[0, at(start, TILE)].astype(F32)
        for k in range(3):
            back = back + dot(grad_two[at(start + (2 - k) * wide, TILE)], weight_t[k])
        grad = (back * slope_one[at(start + LANES, TILE)]).astype(BF16)
        acc[...] += dot(onehot[:16, pl.ds(pl.multiple_of(start + LANES, LANES), TILE)], grad)

    loop(0, tiles, tile_back)
    own_sum[...] = acc[...].astype(BF16)
    to_sum = in_sum.at[q]
    sum_copies = send_all("seq", seq_peers, 1, lambda peer: own_sum, lambda i: to_sum)
    in_sum[q] = own_sum[...]

    for copy in first_copies:
        copy.wait()
    value = mine[q].astype(F32)
    for i in range(along - 1):
        value = value + in_seq[i].astype(F32)
    part[:blocks] = value.astype(BF16)
    if across > blocks + 1:
        part[blocks + 1 :] = jnp.zeros((across - blocks - 1, 16, channels), BF16)
    for copy in sum_copies:
        copy.wait()
    value = in_sum[0].astype(F32)
    for i in range(1, along):
        value = value + in_sum[i].astype(F32)
    part[blocks] = value.astype(BF16)

    copies = send_all("dp", dp_peers, 2, lambda peer: part.at[peer], lambda i: in_dp.at[i])
    for copy in copies:
        copy.wait()
    value = part[d].astype(F32)
    for i in range(across - 1):
        value = value + in_dp[i].astype(F32)
    held[q, d] = value.astype(BF16)

    ready = held.at[q, d]
    copies = send_all("dp", dp_peers, 3, lambda peer: ready, lambda i: ready)
    for copy in copies:
        copy.wait()
    group = held.at[q, pl.ds(0, blocks)]
    copies = send_all("seq", seq_peers, 4, lambda peer: group, lambda i: group)
    for copy in copies:
        copy.wait()
    for i in range(along):
        rows_ref[i] = held[i, :blocks]
    sums_ref[...] = held[q, blocks]
    stored.wait()


def panel(codes, embed, first, second, cot):
    length, channels = cot.shape[1:]
    span = length + 2 * LANES
    across, along = lax.axis_size("dp"), lax.axis_size("seq")
    blocks = pl.cdiv(channels + channels // 2, 16 * along)
    assert blocks < across and length % TILE == 0 and length // TILE >= 4
    sems = []
    for count in (along, along, across, across, along):
        sems += [pltpu.SemaphoreType.DMA((count - 1,))] * 2
    return pl.pallas_call(
        functools.partial(panel_kernel, across, along, blocks),
        out_shape=(
            jax.ShapeDtypeStruct(cot.shape, BF16),
            jax.ShapeDtypeStruct((along, blocks, 16, channels), BF16),
            jax.ShapeDtypeStruct((16, channels), BF16),
        ),
        in_specs=[ANY, ANY, VMEM, ANY, ANY],
        out_specs=(ANY, VMEM, VMEM),
        scratch_shapes=[
            pltpu.VMEM((1, span), jnp.int32),
            pltpu.VMEM(cot.shape, BF16),
            pltpu.VMEM(first.shape, BF16),
            pltpu.VMEM(second.shape, BF16),
            pltpu.VMEM((2, 1, LANES), jnp.int32),
            pltpu.VMEM((2, SECOND_DILATION, channels), BF16),
            pltpu.VMEM((48, span), BF16),
            pltpu.VMEM((span, channels), BF16),
            pltpu.VMEM((span, channels), F32),
            pltpu.VMEM((length + 2 * SECOND_DILATION, channels), BF16),
            pltpu.VMEM((3, channels, channels), BF16),
            pltpu.VMEM((3, channels, channels), BF16),
            pltpu.VMEM((3, channels, channels), F32),
            pltpu.VMEM((16, channels), F32),
            pltpu.VMEM((along, blocks, 16, channels), BF16),
            pltpu.VMEM((16, channels), BF16),
            pltpu.VMEM((along - 1, blocks, 16, channels), BF16),
            pltpu.VMEM((along, 16, channels), BF16),
            pltpu.VMEM((across, 16, channels), BF16),
            pltpu.VMEM((across - 1, 16, channels), BF16),
            pltpu.VMEM((along, across, 16, channels), BF16),
            pltpu.VMEM(cot.shape, BF16),
            pltpu.SemaphoreType.DMA((5,)),
            pltpu.SemaphoreType.DMA((4,)),
            pltpu.SemaphoreType.DMA((4,)),
            *sems,
        ],
        compiler_params=pltpu.CompilerParams(
            collective_id=0, has_side_effects=True, vmem_limit_bytes=60 * 1024 * 1024
        ),
        name="panel",
    )(codes, cot, embed, first, second)


def expand_kernel(x_ref, sums_ref, embed_ref, block_ref, out_ref, first_ref, second_ref, block, done):
    fetch = pltpu.make_async_copy(block_ref, block, done.at[0])
    fetch.start()
    channels = embed_ref.shape[1]
    half = channels // 2
    flip = flip_matrix(channels)
    outer = x_ref[:channels]
    second_ref[0] = outer.astype(F32)
    second_ref[2] = dot(dot(flip, outer).astype(BF16), flip)
    inner = x_ref[channels : channels + half]
    second_ref[1, :half] = inner.astype(F32)
    second_ref[1, half:] = dot(dot(flip[half:, :half], inner).astype(BF16), flip)
    fetch.wait()
    move = pltpu.make_async_copy(block, out_ref, done.at[1])
    move.start()
    sums = sums_ref[...]
    sums_flip = dot(sums, flip).astype(BF16)
    embed = embed_ref[...]
    for k in range(3):
        row = lax.broadcasted_iota(jnp.int32, (16, BASES), 0)
        col = lax.broadcasted_iota(jnp.int32, (16, BASES), 1)
        here = dot((row == BASES * k + col).astype(F32).astype(BF16), embed).astype(BF16)
        there = dot((row == BASES * (2 - k) + col).astype(F32).astype(BF16), embed).astype(BF16)
        there = dot(there, flip).astype(BF16)
        first_ref[k] = dot_rows(here, sums) + dot_rows(there, sums_flip)
    move.wait()


def expand(x, sums, embed, block):
    channels = x.shape[1]
    shape = jax.ShapeDtypeStruct((3, channels, channels), F32)
    return pl.pallas_call(
        expand_kernel,
        out_shape=(jax.ShapeDtypeStruct(block.shape, BF16), shape, shape),
        in_specs=[VMEM, VMEM, VMEM, ANY],
        out_specs=(ANY, VMEM, VMEM),
        scratch_shapes=[pltpu.VMEM(block.shape, BF16), pltpu.SemaphoreType.DMA((2,))],
        compiler_params=pltpu.CompilerParams(vmem_limit_bytes=60 * 1024 * 1024),
        name="expand",
    )(x, sums, embed, block)


def local(codes, embed, first, second, cot):
    block, rows, sums = panel(codes, embed, first, second, cot)
    return expand(rows.reshape(-1, cot.shape[2]), sums, embed, block)


def solution(mesh):
    in_specs = (P("dp", "seq"), P(), P(), P(), P("dp", "seq", None))
    out_specs = (P("dp", "seq", None), P(), P())
    return jax.shard_map(local, mesh=mesh, in_specs=in_specs, out_specs=out_specs, check_vma=False)
```

time: 224 us -> 34.7 us (0.15)
  waiting for transfers between devices: 134 us -> 0 us
  Pallas kernels: 0 us -> 33.8 us
  local copies, waits for them, and re-layouts: 23.7 us -> 0 us
  other arithmetic: 18.3 us -> 0 us
  matrix products: 16.4 us -> 0 us
  starting transfers between devices: 15.9 us -> 0 us
  between operations: 14.4 us -> 0.64 us
    psum x1 -> x0, waiting for transfers between devices: 134 us -> none  [local(): first_weight_gradient = lax.psum(first_weight_gradient, ('dp', 'seq'))]
    pallas_call x0 -> x2, Pallas kernels: none -> 33.8 us  [the longest x1 29.5 us: panel(): pl.pallas_call(functools.partial(panel_kernel, across, along, blocks), ou...]
    dot_general x6 -> x0, matrix products: 16.4 us -> none  [the longest x4 11.1 us: product(): jnp.dot(stacked.reshape(-1, shape_in[-1]), matrix, preferred_element_type...]
    ppermute x6 -> x0, starting transfers between devices: 15.9 us -> none  [the longest x3 11.8 us: with_halo(): lax.ppermute(tail, axis, [(i, (i + 1) % count) for i in range(ends)])]
    dot_general x2 -> x0, other arithmetic: 12.2 us -> none  [weight_term(): jnp.dot(stacked.reshape(-1, 3 * channels).T, grad.reshape(-1, channels),...]
    rev x4 -> x0, local copies, waits for them, and re-layouts: 8.8 us -> none  [the longest x2 6.64 us: layer_forward_pass(): reversed_taps = weight[::-1, ::-1, ::-1].reshape(-1, channels)]
    unnamed x41 -> x0, local copies, waits for them, and re-layouts: 7.38 us -> none
    dot_general x2 -> x0, local copies, waits for them, and re-layouts: 5.97 us -> none  [weight_term(): jnp.dot(stacked.reshape(-1, 3 * channels).T, grad.reshape(-1, channels),...]
  transfers between devices with their start and end apart: 7 -> 0, of which waited for: 1 -> 0; matrix products, arithmetic and copies ran while one was open for 14% -> 0% of each run, Pallas kernels for 0% -> 0%
where the time goes in v2:
time: 34.7 us; the launch traced here: 34.5 us
  Pallas kernels  33.8 us (97%)
  between operations  0.64 us (2%)
    pallas_call x1, Pallas kernels, panel(): pl.pallas_call(functools.partial(panel_kernel, across, along, blocks), ou...  29.5 us
    pallas_call x1, Pallas kernels, expand(): pl.pallas_call(expand_kernel, out_shape=(jax.ShapeDtypeStruct(block.shape...  4.3 us

profile of v2, /device:TPU:0, one launch (start us, length us, event | category | flops | bytes accessed | tf_op | source)
XLA Modules:
  0.0 34.5 jit_solution(10847831617144223435)
XLA Ops:
  0.6 29.5 %panel.1 = (bf16[1,2048,256]{2,1,0:T(8,128)(2,1)}, bf16[4,6,16,256]{3,2,1,0:T(8,128)(2,1)}, bf16[16,256]{1,0:T(8,128)(2,1)}) custom-call(s32[1,2048]{1,0:T(1,128)} %codes_ref.1, bf16[1,2048,256]{2,1,0:T(8,128)(2,1)} %cot_ref.1, bf16[4,256]{1,0:T(4,128)(2,1)} %embed_ref.3, bf16[3,256,256]{2,1,0:T(8,128)(2,1)} %first_ref.1, bf16[3,256,256]{2,1,0:T(8,128)(2,1)} %second_ref.1), custom_call_target="tpu_custom_call" | custom-call | tf_op jit(solution)/shard_map/panel/pallas_call | solution.py:303
  30.2 4.3 %expand.1 = (bf16[1,2048,256]{2,1,0:T(8,128)(2,1)}, f32[3,256,256]{2,1,0:T(8,128)}, f32[3,256,256]{2,1,0:T(8,128)}) custom-call(bf16[384,256]{1,0:T(8,128)(2,1)} %bitcast.1, bf16[16,256]{1,0:T(8,128)(2,1)} %get-tuple-element.7.sums_ref, bf16[4,256]{1,0:T(4,128)(2,1)} %embed_ref.3, bf16[1,2048,256]{2,1,0:T(8,128)(2,1)} %get-tuple-element.8.block_ref), custom_call_target="tpu_custom_call" | custom-call | tf_op jit(solution)/shard_map/expand/pallas_call | solution.py:378

commit v3 on v2

--- a/solution.py
+++ b/solution.py
@@ -50,7 +50,7 @@
     codes_ref, cot_ref, embed_ref, first_ref, second_ref,
     block_ref, rows_ref, sums_ref,
     ext, cot, first, second, code_in, cot_in, onehot, hidden, slope_one, grad_two,
-    weight, weight_t, total, acc, mine, own_sum, in_seq, in_sum, part, in_dp, held, block,
+    weight, weight_t, total, acc, mine, own_sum, in_seq, in_sum, part, in_dp, held,
     load, halo_send, halo_recv, *sems,
 ):
     d, q = lax.axis_index("dp"), lax.axis_index("seq")
@@ -177,7 +177,7 @@
         start = i * TILE
         value = layer_two(start, TILE, cot[0, at(start, TILE)])
         value = hidden[at(start + LANES, TILE)].astype(F32) + value
-        block[0, at(start, TILE)] = value.astype(BF16)
+        block_ref[0, at(start, TILE)] = value.astype(BF16)
 
     def loop(first, last, body):
         if last > first:
@@ -205,9 +205,6 @@
     for i in (0, 1, tiles - 2, tiles - 1):
         tile_two(i)
 
-    stored = pltpu.make_async_copy(block, block_ref, load.at[4])
-    stored.start()
-
     total[...] = jnp.zeros_like(total)
 
     def tile_terms(i):
@@ -288,7 +285,6 @@
     for i in range(along):
         rows_ref[i] = held[i, :blocks]
     sums_ref[...] = held[q, blocks]
-    stored.wait()
 
 
 def panel(codes, embed, first, second, cot):
@@ -303,12 +299,12 @@
     return pl.pallas_call(
         functools.partial(panel_kernel, across, along, blocks),
         out_shape=(
-            jax.ShapeDtypeStruct(cot.shape, BF16),
-            jax.ShapeDtypeStruct((along, blocks, 16, channels), BF16),
-            jax.ShapeDtypeStruct((16, channels), BF16),
+            pltpu.VMEM(cot.shape, BF16),
+            pltpu.VMEM((along, blocks, 16, channels), BF16),
+            pltpu.VMEM((16, channels), BF16),
         ),
         in_specs=[ANY, ANY, VMEM, ANY, ANY],
-        out_specs=(ANY, VMEM, VMEM),
+        out_specs=(VMEM, VMEM, VMEM),
         scratch_shapes=[
             pltpu.VMEM((1, span), jnp.int32),
             pltpu.VMEM(cot.shape, BF16),
@@ -331,8 +327,7 @@
             pltpu.VMEM((across, 16, channels), BF16),
             pltpu.VMEM((across - 1, 16, channels), BF16),
             pltpu.VMEM((along, across, 16, channels), BF16),
-            pltpu.VMEM(cot.shape, BF16),
-            pltpu.SemaphoreType.DMA((5,)),
+            pltpu.SemaphoreType.DMA((4,)),
             pltpu.SemaphoreType.DMA((4,)),
             pltpu.SemaphoreType.DMA((4,)),
             *sems,
@@ -344,21 +339,27 @@
     )(codes, cot, embed, first, second)
 
 
-def expand_kernel(x_ref, sums_ref, embed_ref, block_ref, out_ref, first_ref, second_ref, block, done):
-    fetch = pltpu.make_async_copy(block_ref, block, done.at[0])
-    fetch.start()
+def expand_kernel(x_ref, sums_ref, embed_ref, block_ref, out_ref, first_out, second_out, first_ref, second_ref, done):
+    moves = []
+
+    def move(src, dst):
+        copy = pltpu.make_async_copy(src, dst, done.at[len(moves)])
+        copy.start()
+        moves.append(copy)
+
+    move(block_ref, out_ref)
     channels = embed_ref.shape[1]
     half = channels // 2
     flip = flip_matrix(channels)
     outer = x_ref[:channels]
     second_ref[0] = outer.astype(F32)
+    move(second_ref.at[0], second_out.at[0])
     second_ref[2] = dot(dot(flip, outer).astype(BF16), flip)
+    move(second_ref.at[2], second_out.at[2])
     inner = x_ref[channels : channels + half]
     second_ref[1, :half] = inner.astype(F32)
     second_ref[1, half:] = dot(dot(flip[half:, :half], inner).astype(BF16), flip)
-    fetch.wait()
-    move = pltpu.make_async_copy(block, out_ref, done.at[1])
-    move.start()
+    move(second_ref.at[1], second_out.at[1])
     sums = sums_ref[...]
     sums_flip = dot(sums, flip).astype(BF16)
     embed = embed_ref[...]
@@ -369,7 +370,9 @@
         there = dot((row == BASES * (2 - k) + col).astype(F32).astype(BF16), embed).astype(BF16)
         there = dot(there, flip).astype(BF16)
         first_ref[k] = dot_rows(here, sums) + dot_rows(there, sums_flip)
-    move.wait()
+        move(first_ref.at[k], first_out.at[k])
+    for copy in moves:
+        copy.wait()
 
 
 def expand(x, sums, embed, block):
@@ -378,10 +381,14 @@
     return pl.pallas_call(
         expand_kernel,
         out_shape=(jax.ShapeDtypeStruct(block.shape, BF16), shape, shape),
-        in_specs=[VMEM, VMEM, VMEM, ANY],
-        out_specs=(ANY, VMEM, VMEM),
-        scratch_shapes=[pltpu.VMEM(block.shape, BF16), pltpu.SemaphoreType.DMA((2,))],
-        compiler_params=pltpu.CompilerParams(vmem_limit_bytes=60 * 1024 * 1024),
+        in_specs=[VMEM, VMEM, VMEM, VMEM],
+        out_specs=(ANY, ANY, ANY),
+        scratch_shapes=[
+            pltpu.VMEM(shape.shape, F32),
+            pltpu.VMEM(shape.shape, F32),
+            pltpu.SemaphoreType.DMA((7,)),
+        ],
+        compiler_params=pltpu.CompilerParams(vmem_limit_bytes=32 * 1024 * 1024),
         name="expand",
     )(x, sums, embed, block)
 

time: 34.7 us -> 32.1 us (0.925)
  Pallas kernels: 33.8 us -> 30.6 us
  local copies, waits for them, and re-layouts: 0 us -> 0.68 us
    pallas_call x1, Pallas kernels: 4.3 us -> 1.8 us  [expand(): pl.pallas_call(expand_kernel, out_shape=(jax.ShapeDtypeStruct(block.shape...]
    pallas_call x1, Pallas kernels: 29.5 us -> 28.8 us  [panel(): pl.pallas_call(functools.partial(panel_kernel, across, along, blocks), ou...]
    unnamed x0 -> x2, local copies, waits for them, and re-layouts: none -> 0.68 us
where the time goes in v3:
time: 32.1 us; the launch traced here: 32 us
  Pallas kernels  30.6 us (95%)
  local copies, waits for them, and re-layouts  0.68 us (2%)
  between operations  0.65 us (2%)
    pallas_call x1, Pallas kernels, panel(): pl.pallas_call(functools.partial(panel_kernel, across, along, blocks), ou...  28.8 us
    pallas_call x1, Pallas kernels, expand(): pl.pallas_call(expand_kernel, out_shape=(jax.ShapeDtypeStruct(block.shape...  1.8 us
    unnamed x2, local copies, waits for them, and re-layouts  0.68 us

profile of v3, /device:TPU:0, one launch (start us, length us, event | category | flops | bytes accessed | tf_op | source)
XLA Modules:
  0.0 32.0 jit_solution(8382586729102040102)
XLA Ops:
  0.6 28.8 %panel.1 = (bf16[1,2048,256]{2,1,0:T(8,128)(2,1)S(1)}, bf16[4,6,16,256]{3,2,1,0:T(8,128)(2,1)S(1)}, bf16[16,256]{1,0:T(8,128)(2,1)S(1)}) custom-call(s32[1,2048]{1,0:T(1,128)} %codes_ref.1, bf16[1,2048,256]{2,1,0:T(8,128)(2,1)} %cot_ref.1, bf16[4,256]{1,0:T(4,128)(2,1)} %embed_ref.3, bf16[3,256,256]{2,1,0:T(8,128)(2,1)} %first_ref.1, ...), custom_call_target="tpu_custom_call" | custom-call | tf_op jit(solution)/shard_map/panel/pallas_call | solution.py:299
  29.5 0.0 copy-start
  29.5 0.7 %copy-done = bf16[4,256]{1,0:T(4,128)(2,1)S(1)} copy-done((bf16[4,256]{1,0:T(4,128)(2,1)S(1)}, bf16[4,256]{1,0:T(4,128)(2,1)}, u32[]{:S(2)}) %copy-start) | copy-done | bytes 2072
  30.2 1.8 %expand.1 = (bf16[1,2048,256]{2,1,0:T(8,128)(2,1)}, f32[3,256,256]{2,1,0:T(8,128)}, f32[3,256,256]{2,1,0:T(8,128)}) custom-call(bf16[384,256]{1,0:T(8,128)(2,1)S(1)} %bitcast.1, bf16[16,256]{1,0:T(8,128)(2,1)S(1)} %get-tuple-element.7.sums_ref, bf16[4,256]{1,0:T(4,128)(2,1)S(1)} %copy-done, bf16[1,2048,256]{2,1,0:T(8,128)(2,1)S(1)} %get-tuple-element.8.block_ref), custom_call_target="tpu_custom_call" | custom-call | tf_op jit(solution)/shard_map/expand/pallas_call | solution.py:381
Async XLA Ops:
  29.5 0.7 %copy-start = (bf16[4,256]{1,0:T(4,128)(2,1)S(1)}, bf16[4,256]{1,0:T(4,128)(2,1)}, u32[]{:S(2)}) copy-start(bf16[4,256]{1,0:T(4,128)(2,1)} %embed_ref.3) | copy-start | bytes 6148
